TPU v7x, 32 devices: a whole 2x2x4 slice. The times are simulated.
32 devices in a mesh: ctx: 4 (over z), head: 8 (over y, x, core).
Axes of the slice: x: 2, y: 2, z: 4, core: 2. Of those that a mesh axis runs over, the one named last changes fastest.
Arguments:
- queries: bfloat16 [12288, 4096], P('ctx', 'head'), may hold values from -64 to 64
- key_vectors: bfloat16 [12288, 4096], P('ctx', 'head'), may hold values from -5 to 5
- value_vectors: bfloat16 [12288, 4096], P('ctx', 'head'), may hold values from -6 to 6
- step_sizes: float32 [8, 12288], P('head', 'ctx'), may hold values from 0.0003 to 0.003
- w_in: bfloat16 [8, 512, 512], P('head'), may hold values from -0.25 to 0.25
- w_up: bfloat16 [8, 512, 512], P('head'), may hold values from -0.25 to 0.25
- w_out: bfloat16 [8, 512, 512], P('head'), may hold values from -0.125 to 0.125
- out_gate: bfloat16 [12288, 4096], P('ctx', 'head'), may hold values from -6 to 6
- norm_gain: float32 [4096], replicated, may hold values from 0.5 to 1.5
Outputs:
- layer_out: bfloat16 [12288, 4096], P(('ctx', 'head'))
All inputs are finite; a program needn't handle non-finite values.
Results may differ from a plain program's by a relative error of at most 0.025.
Values may be sent and summed in bfloat16 or wider, within the bound.
A program may use at most 128 MiB of HBM per device.

v0:
```python
import functools
import math

import jax
import jax.numpy as jnp
from jax import lax
from jax.experimental import pallas as pl
from jax.experimental.pallas import tpu as pltpu
from jax.sharding import PartitionSpec as P

WINDOW = 1024
EPSILON = 1e-06
BQ = 256
PW = 128
F32 = jnp.float32
BF16 = jnp.bfloat16
NT = (((1,), (1,)), ((), ()))
TN = (((0,), (0,)), ((), ()))


def dotf(a, b, dims=None):
    if dims is None:
        return jnp.dot(a, b, preferred_element_type=F32)
    return lax.dot_general(a, b, dims, preferred_element_type=F32)


def as_column(row, width=128):
    return jnp.transpose(jnp.broadcast_to(row, (width, row.shape[1])))


def as_row(column):
    return jnp.transpose(jnp.broadcast_to(column, (column.shape[0], 128)))[:1]


def wide(x, width):
    return jnp.concatenate([x] * (width // x.shape[1]), axis=1)


def masked(scores, head_mask, tail_mask):
    row = lax.broadcasted_iota(jnp.int32, (BQ, BQ), 0)
    col = lax.broadcasted_iota(jnp.int32, (BQ, BQ), 1)
    width = scores.shape[1]
    parts = []
    low, high = 0, width
    if head_mask:
        parts.append(jnp.where(col > row, scores[:, :BQ], -1e30))
        low = BQ
    if tail_mask:
        high = width - BQ
    if high > low:
        parts.append(scores[:, low:high])
    if tail_mask:
        parts.append(jnp.where(col <= row, scores[:, high:], -1e30))
    return parts[0] if len(parts) == 1 else jnp.concatenate(parts, axis=1)


def attend(q, k, v, head_mask, tail_mask):
    scale = math.log2(math.e) * q.shape[1] ** (-0.5)
    s = masked(dotf(q, k, NT), head_mask, tail_mask)
    m = jnp.max(s, axis=1, keepdims=True)
    p = jnp.exp2((s - m) * scale)
    l = jnp.sum(p, axis=1, keepdims=True)
    return dotf(p.astype(BF16), v), m, l


def kernel(
    n_ctx, n_head, rows, hd, fh,
    q_hbm, k_hbm, v_hbm, step_ref, win_hbm, wup_hbm, wout_hbm, gate_hbm, gain_ref,
    out_hbm,
    q_ref, k_ref, v_ref, gate_ref, w_ref, new_ref,
    acc_ref, own_ref, rin_ref, lin_ref, rout_ref, lout_ref,
    att_ref, stat_ref, gq_ref, go_ref, gst_ref, oin_ref, ost_ref,
    z_ref, ss_ref, land_ref, sland_ref,
    load_sem, rsend, rrecv, lsend, lrecv, hsend, hrecv, asend, arecv, ssend, srecv, own_sem, out_sem,
):
    ci = lax.axis_index("ctx")
    hi = lax.axis_index("head")
    first, last = ci == 0, ci == n_ctx - 1
    not_first, not_last = ci > 0, ci < n_ctx - 1
    per = rows // n_head
    pieces = 3 * fh // PW
    width = fh // 2
    per_half = width // PW
    halo_blocks = WINDOW // BQ
    scale = math.log2(math.e) * hd ** (-0.5)

    loads = [
        pltpu.make_async_copy(win_hbm.at[0], w_ref.at[0], load_sem.at[0]),
        pltpu.make_async_copy(wup_hbm.at[0], w_ref.at[1], load_sem.at[1]),
        pltpu.make_async_copy(wout_hbm.at[0], w_ref.at[2], load_sem.at[2]),
        pltpu.make_async_copy(k_hbm, k_ref, load_sem.at[3]),
        pltpu.make_async_copy(v_hbm, v_ref, load_sem.at[4]),
        pltpu.make_async_copy(q_hbm, q_ref, load_sem.at[5]),
        pltpu.make_async_copy(gate_hbm, gate_ref, load_sem.at[6]),
    ]
    for load in loads:
        load.start()

    barrier = pltpu.get_barrier_semaphore()

    @pl.when(not_first)
    def _():
        pl.semaphore_signal(barrier, inc=1, device_id={"ctx": ci - 1})

    @pl.when(not_last)
    def _():
        pl.semaphore_signal(barrier, inc=1, device_id={"ctx": ci + 1})

    @pl.loop(1, n_head)
    def _(s):
        pl.semaphore_signal(barrier, inc=1, device_id={"head": lax.rem(hi + s, n_head)})

    pl.semaphore_wait(barrier, n_head - 1 + jnp.where(first, 0, 1) + jnp.where(last, 0, 1))

    def q_back():
        return pltpu.make_async_remote_copy(
            src_ref=q_hbm.at[pl.ds(0, WINDOW)], dst_ref=gq_ref, send_sem=hsend.at[0],
            recv_sem=hrecv.at[0], device_id={"ctx": ci - 1})

    def o_forward():
        return pltpu.make_async_remote_copy(
            src_ref=go_ref, dst_ref=oin_ref, send_sem=hsend.at[1],
            recv_sem=hrecv.at[1], device_id={"ctx": ci + 1})

    def st_forward():
        return pltpu.make_async_remote_copy(
            src_ref=gst_ref, dst_ref=ost_ref, send_sem=hsend.at[2],
            recv_sem=hrecv.at[2], device_id={"ctx": ci + 1})

    def to_right(p):
        return pltpu.make_async_remote_copy(
            src_ref=rout_ref.at[p], dst_ref=rin_ref.at[p], send_sem=rsend.at[p],
            recv_sem=rrecv.at[p], device_id={"ctx": ci + 1})

    def to_left(p):
        return pltpu.make_async_remote_copy(
            src_ref=lout_ref.at[p], dst_ref=lin_ref.at[p], send_sem=lsend.at[p],
            recv_sem=lrecv.at[p], device_id={"ctx": ci - 1})

    @pl.when(not_first)
    def _():
        q_back().start()

    for load in loads[:5]:
        load.wait()

    tb = rows // 4

    def increments(half):
        cols = pl.ds(half * width, width)
        acc_ref[...] = jnp.zeros_like(acc_ref)

        @pl.loop(0, rows // tb)
        def _(block):
            start = pl.multiple_of(block * tb, tb)
            span = pl.ds(start, tb)
            k = k_ref[span, :]
            rate = as_column(step_ref[:, span])
            scaled = (wide(rate, hd) * v_ref[span, :].astype(F32)).astype(BF16)
            gate = dotf(k, w_ref[0, :, cols])
            up = dotf(k, w_ref[1, :, cols])
            back = dotf(scaled, w_ref[2, :, cols])
            sig = jax.nn.sigmoid(gate)
            silu = gate * sig
            hidden = (silu * up).astype(BF16)
            g_gate = (back * up * (sig * (1.0 + gate * (1.0 - sig)))).astype(BF16)
            g_up = (back * silu).astype(BF16)
            acc_ref[:, : 2 * width] += dotf(k, jnp.concatenate([g_gate, g_up], axis=1), TN)
            acc_ref[:, 2 * width :] += dotf(scaled, hidden, TN)

        for x in range(3):
            for part in range(per_half):
                p = (half * 3 + x) * per_half + part
                base = x * width + part * PW
                piece = acc_ref[:, base : base + PW].astype(BF16)
                own_ref[p] = piece

                @pl.when(first)
                def _():
                    rout_ref[p] = piece
                    rin_ref[p] = jnp.zeros_like(piece)
                    to_right(p).start()

                @pl.when(last)
                def _():
                    lout_ref[p] = piece
                    lin_ref[p] = jnp.zeros_like(piece)
                    to_left(p).start()

    def chain(t):
        pr = t - (ci - 1)
        pleft = t - (n_ctx - 2 - ci)
        pd = t - (n_ctx - 2)

        @pl.when(not_first & (pr >= 0) & (pr < pieces))
        def _():
            to_right(pr).wait_recv()

            @pl.when(not_last)
            def _():
                rout_ref[pr] = (rin_ref[pr].astype(F32) + own_ref[pr].astype(F32)).astype(BF16)
                to_right(pr).start()

        @pl.when(not_last & (pleft >= 0) & (pleft < pieces))
        def _():
            to_left(pleft).wait_recv()

            @pl.when(not_first)
            def _():
                lout_ref[pleft] = (lin_ref[pleft].astype(F32) + own_ref[pleft].astype(F32)).astype(BF16)
                to_left(pleft).start()

        @pl.when((pd >= 0) & (pd < pieces))
        def _():
            x = lax.rem(pd // per_half, 3)
            col = (pd // (3 * per_half)) * width + lax.rem(pd, per_half) * PW
            cols = pl.ds(pl.multiple_of(col, PW), PW)
            before = w_ref[x, :, cols].astype(F32)
            total = own_ref[pd].astype(F32) + rin_ref[pd].astype(F32) + lin_ref[pd].astype(F32)
            after = before + total
            rescale = jnp.sqrt(jnp.mean(before * before, axis=0, keepdims=True) + EPSILON) / jnp.sqrt(
                jnp.mean(after * after, axis=0, keepdims=True) + EPSILON)
            new_ref[x, :, cols] = (after * rescale).astype(BF16)

    for half in range(2):
        increments(half)
    loads[5].wait()

    n_blocks = rows // BQ

    @pl.loop(halo_blocks, n_blocks)
    def _(b):
        start = pl.multiple_of(b * BQ, BQ)
        keys = pl.ds(pl.multiple_of(start - WINDOW, BQ), WINDOW + BQ)
        o, _, l = attend(q_ref[pl.ds(start, BQ), :], k_ref[keys, :], v_ref[keys, :], True, True)
        att_ref[pl.ds(start, BQ), :] = o / l
        chain(b - halo_blocks)

    t = n_blocks - halo_blocks
    for b in range(halo_blocks):
        span = pl.ds(b * BQ, BQ)
        keys = pl.ds(0, (b + 1) * BQ)
        o, m, l = attend(q_ref[span, :], k_ref[keys, :], v_ref[keys, :], False, True)
        att_ref[span, :] = o
        stat_ref[0, span, :] = jnp.broadcast_to(m, (BQ, 128))
        stat_ref[1, span, :] = jnp.broadcast_to(l, (BQ, 128))
        chain(t + b)
    t += halo_blocks

    @pl.when(not_last)
    def _():
        q_back().wait_recv()
        for b in range(halo_blocks):
            span = pl.ds(b * BQ, BQ)
            keys = pl.ds(rows - WINDOW + b * BQ, WINDOW - b * BQ)
            o, m, l = attend(gq_ref[span, :], k_ref[keys, :], v_ref[keys, :], True, False)
            go_ref[span, :] = o.astype(BF16)
            gst_ref[b] = jnp.concatenate([as_row(m), as_row(l), jnp.zeros((6, BQ), F32)], axis=0)
        o_forward().start()
        st_forward().start()

    @pl.loop(t, pieces + n_ctx - 2)
    def _(step):
        chain(step)

    loads[6].wait()

    @pl.when(first)
    def _():
        oin_ref[...] = jnp.zeros_like(oin_ref)
        ost_ref[...] = jnp.full_like(ost_ref, -1e30)

    gain = gain_ref[:, pl.ds(pl.multiple_of(hi * hd, hd), hd)]

    def rows_to(d):
        return pltpu.make_async_remote_copy(
            src_ref=z_ref.at[d], dst_ref=land_ref.at[hi], send_sem=asend.at[d],
            recv_sem=arecv.at[hi], device_id={"head": d})

    def squares_to(d):
        return pltpu.make_async_remote_copy(
            src_ref=ss_ref.at[d], dst_ref=sland_ref.at[hi], send_sem=ssend.at[d],
            recv_sem=srecv.at[hi], device_id={"head": d})

    def rows_from(s):
        return pltpu.make_async_remote_copy(
            src_ref=z_ref.at[s], dst_ref=land_ref.at[s], send_sem=asend.at[s],
            recv_sem=arecv.at[s], device_id={"head": s})

    def squares_from(s):
        return pltpu.make_async_remote_copy(
            src_ref=ss_ref.at[s], dst_ref=sland_ref.at[s], send_sem=ssend.at[s],
            recv_sem=srecv.at[s], device_id={"head": s})

    padded = ss_ref.shape[2]

    def apply(d):
        span = pl.ds(pl.multiple_of(d * per, 64), per)
        q = q_ref[span, :]
        gate = dotf(q, new_ref[0])
        up = dotf(q, new_ref[1])
        hidden = (jax.nn.silu(gate) * up).astype(BF16)
        combined = (att_ref[span, :] + dotf(hidden, new_ref[2], NT)).astype(BF16).astype(F32)
        og = gate_ref[span, :].astype(F32)
        z_ref[d] = (combined * gain * jax.nn.silu(og)).astype(BF16)
        square = (combined * combined).astype(BF16)
        if padded > per:
            square = jnp.concatenate([square, jnp.zeros((padded - per, hd), BF16)], axis=0)
        ss_ref[d] = dotf(jnp.ones((8, hd), BF16), square, NT)

        @pl.when(d != hi)
        def _():
            rows_to(d).start()
            squares_to(d).start()

    halo_chunks = -(-WINDOW // per)
    rest = n_head - halo_chunks

    @pl.loop(0, rest)
    def _(s):
        apply(halo_chunks + lax.rem(hi + s, rest))

    @pl.when(not_first)
    def _():
        o_forward().wait_recv()
        st_forward().wait_recv()

    for b in range(halo_blocks):
        span = pl.ds(b * BQ, BQ)
        m1, l1 = stat_ref[0, span, :], stat_ref[1, span, :]
        m2, l2 = as_column(ost_ref[b, :1]), as_column(ost_ref[b, 1:2])
        l2 = jnp.where(m2 > -1e29, l2, 0.0)
        m = jnp.maximum(m1, m2)
        e1 = jnp.exp2((m1 - m) * scale)
        e2 = jnp.exp2((m2 - m) * scale)
        inverse = 1.0 / (l1 * e1 + l2 * e2)
        att_ref[span, :] = att_ref[span, :] * wide(e1 * inverse, hd) + oin_ref[span, :].astype(F32) * wide(
            e2 * inverse, hd)

    @pl.loop(0, halo_chunks)
    def _(s):
        apply(lax.rem(hi + s, halo_chunks))

    own = pltpu.make_async_copy(z_ref.at[hi], land_ref.at[hi], own_sem.at[0])
    own.start()
    own_squares = pltpu.make_async_copy(ss_ref.at[hi], sland_ref.at[hi], own_sem.at[1])
    own_squares.start()
    own.wait()
    own_squares.wait()

    @pl.loop(1, n_head)
    def _(s):
        squares_from(lax.rem(hi + s, n_head)).wait_recv()

    total = sland_ref[0]
    for s in range(1, n_head):
        total = total + sland_ref[s]
    inv = lax.rsqrt(as_column(total[:1])[:per] * (1.0 / (n_head * hd)) + EPSILON)
    inv = wide(inv, hd)

    @pl.loop(1, n_head)
    def _(s):
        rows_from(lax.rem(hi + s, n_head)).wait_recv()

    @pl.loop(1, n_head)
    def _(s):
        d = lax.rem(hi + s, n_head)
        rows_to(d).wait_send()
        squares_to(d).wait_send()

    for s in range(n_head):
        z_ref[s] = (land_ref[s].astype(F32) * inv).astype(BF16)
        pltpu.make_async_copy(z_ref.at[s], out_hbm.at[:, pl.ds(s * hd, hd)], out_sem.at[s]).start()
    for s in range(n_head):
        pltpu.make_async_copy(z_ref.at[s], out_hbm.at[:, pl.ds(s * hd, hd)], out_sem.at[s]).wait()

    @pl.when(not_first)
    def _():
        q_back().wait_send()

        @pl.loop(0, pieces)
        def _(p):
            to_left(p).wait_send()

    @pl.when(not_last)
    def _():
        o_forward().wait_send()
        st_forward().wait_send()

        @pl.loop(0, pieces)
        def _(p):
            to_right(p).wait_send()


def per_device(q, k, v, steps, w_in, w_up, w_out, out_gate, norm_gain):
    n_ctx, n_head = lax.axis_size("ctx"), lax.axis_size("head")
    rows, hd = q.shape
    fh = w_in.shape[2]
    per = rows // n_head
    padded = -(-per // 128) * 128
    pieces = 3 * fh // PW
    halo_blocks = WINDOW // BQ
    any_spec = pl.BlockSpec(memory_space=pl.ANY)
    vmem = pl.BlockSpec(memory_space=pltpu.VMEM)
    V = pltpu.VMEM
    D = pltpu.SemaphoreType.DMA
    return pl.pallas_call(
        functools.partial(kernel, n_ctx, n_head, rows, hd, fh),
        out_shape=jax.ShapeDtypeStruct((per, n_head * hd), BF16),
        in_specs=[any_spec] * 3 + [vmem] + [any_spec] * 4 + [vmem],
        out_specs=any_spec,
        scratch_shapes=[
            V((rows, hd), BF16), V((rows, hd), BF16), V((rows, hd), BF16), V((rows, hd), BF16),
            V((3, hd, fh), BF16), V((3, hd, fh), BF16),
            V((hd, 3 * fh // 2), F32),
            V((pieces, hd, PW), BF16), V((pieces, hd, PW), BF16), V((pieces, hd, PW), BF16),
            V((pieces, hd, PW), BF16), V((pieces, hd, PW), BF16),
            V((rows, hd), F32), V((2, WINDOW, 128), F32),
            V((WINDOW, hd), BF16), V((WINDOW, hd), BF16), V((halo_blocks, 8, BQ), F32),
            V((WINDOW, hd), BF16), V((halo_blocks, 8, BQ), F32),
            V((n_head, per, hd), BF16), V((n_head, 8, padded), F32),
            V((n_head, per, hd), BF16), V((n_head, 8, padded), F32),
            D((7,)), D((pieces,)), D((pieces,)), D((pieces,)), D((pieces,)), D((3,)), D((3,)),
            D((n_head,)), D((n_head,)), D((n_head,)), D((n_head,)), D((2,)), D((n_head,)),
        ],
        compiler_params=pltpu.CompilerParams(
            collective_id=0, has_side_effects=True, vmem_limit_bytes=58 * 1024 * 1024),
    )(q, k, v, steps, w_in, w_up, w_out, out_gate, norm_gain.reshape(1, -1))


def solution(mesh):
    return jax.shard_map(
        per_device,
        mesh=mesh,
        in_specs=(
            P("ctx", "head"),
            P("ctx", "head"),
            P("ctx", "head"),
            P("head", "ctx"),
            P("head", None, None),
            P("head", None, None),
            P("head", None, None),
            P("ctx", "head"),
            P(),
        ),
        out_specs=P(("ctx", "head"), None),
        check_vma=False,
    )
```

profile of v0, /device:TPU:24, one launch (start us, length us, event | category | flops | bytes accessed | tf_op | source)
XLA Modules:
  0.0 145.1 jit_solution(17453959727432188144)
XLA Ops:
  0.0 141.1 %shard_map.91 = bf16[384,4096]{1,0:T(8,128)(2,1)} custom-call(bf16[3072,512]{1,0:T(8,128)(2,1)} %q_hbm.1, bf16[3072,512]{1,0:T(8,128)(2,1)} %k_hbm.1, bf16[3072,512]{1,0:T(8,128)(2,1)} %v_hbm.1, f32[1,3072]{1,0:T(1,128)} %step_ref.1, bf16[1,512,512]{2,1,0:T(8,128)(2,1)} %win_hbm.1, bf16[1,512,512]{2,1,0:T(8,128)(2,1)} %wup_hbm.1, ...), custom_call_target="tpu_custom_call" | custom-call | tf_op jit(solution)/shard_map/pallas_call | solution.py:407
  141.1 3.9 %copy.11 = bf16[384,4096]{1,0:T(8,128)(2,1)} copy(bf16[384,4096]{1,0:T(8,128)(2,1)} %shard_map.91) | data formatting | bytes 6291456
where the time goes:
time: 145 us
  Pallas kernels  141 us (97%)
  local copies, waits for them, and re-layouts  3.91 us (3%)
    pallas_call x1, Pallas kernels, per_device(): pl.pallas_call(functools.partial(kernel, n_ctx, n_head, rows, hd, fh), ou...  141 us
    unnamed x1, local copies, waits for them, and re-layouts  3.91 us

commit v1 on v0

--- a/solution.py
+++ b/solution.py
@@ -68,7 +68,7 @@
     q_hbm, k_hbm, v_hbm, step_ref, win_hbm, wup_hbm, wout_hbm, gate_hbm, gain_ref,
     out_hbm,
     q_ref, k_ref, v_ref, gate_ref, w_ref, new_ref,
-    acc_ref, own_ref, rin_ref, lin_ref, rout_ref, lout_ref,
+    g_ref, h_ref, scaled_ref, acc_ref, own_ref, rin_ref, lin_ref, rout_ref, lout_ref,
     att_ref, stat_ref, gq_ref, go_ref, gst_ref, oin_ref, ost_ref,
     z_ref, ss_ref, land_ref, sland_ref,
     load_sem, rsend, rrecv, lsend, lrecv, hsend, hrecv, asend, arecv, ssend, srecv, own_sem, out_sem,
@@ -112,20 +112,24 @@
 
     pl.semaphore_wait(barrier, n_head - 1 + jnp.where(first, 0, 1) + jnp.where(last, 0, 1))
 
-    def q_back():
-        return pltpu.make_async_remote_copy(
-            src_ref=q_hbm.at[pl.ds(0, WINDOW)], dst_ref=gq_ref, send_sem=hsend.at[0],
-            recv_sem=hrecv.at[0], device_id={"ctx": ci - 1})
-
-    def o_forward():
-        return pltpu.make_async_remote_copy(
-            src_ref=go_ref, dst_ref=oin_ref, send_sem=hsend.at[1],
-            recv_sem=hrecv.at[1], device_id={"ctx": ci + 1})
-
-    def st_forward():
-        return pltpu.make_async_remote_copy(
-            src_ref=gst_ref, dst_ref=ost_ref, send_sem=hsend.at[2],
-            recv_sem=hrecv.at[2], device_id={"ctx": ci + 1})
+    def q_back(b):
+        span = pl.ds(b * BQ, BQ)
+        return pltpu.make_async_remote_copy(
+            src_ref=q_hbm.at[span], dst_ref=gq_ref.at[span], send_sem=hsend.at[b],
+            recv_sem=hrecv.at[b], device_id={"ctx": ci - 1})
+
+    def o_forward(b):
+        span = pl.ds(b * BQ, BQ)
+        sem = halo_blocks + b
+        return pltpu.make_async_remote_copy(
+            src_ref=go_ref.at[span], dst_ref=oin_ref.at[span], send_sem=hsend.at[sem],
+            recv_sem=hrecv.at[sem], device_id={"ctx": ci + 1})
+
+    def st_forward(b):
+        sem = 2 * halo_blocks + b
+        return pltpu.make_async_remote_copy(
+            src_ref=gst_ref.at[b], dst_ref=ost_ref.at[b], send_sem=hsend.at[sem],
+            recv_sem=hrecv.at[sem], device_id={"ctx": ci + 1})
 
     def to_right(p):
         return pltpu.make_async_remote_copy(
@@ -137,38 +141,60 @@
             src_ref=lout_ref.at[p], dst_ref=lin_ref.at[p], send_sem=lsend.at[p],
             recv_sem=lrecv.at[p], device_id={"ctx": ci - 1})
 
+    early = range(halo_blocks - 1, halo_blocks // 2 - 1, -1)
+    late = range(halo_blocks // 2 - 1, -1, -1)
+
     @pl.when(not_first)
     def _():
-        q_back().start()
+        for b in early:
+            q_back(b).start()
 
     for load in loads[:5]:
         load.wait()
 
     tb = rows // 4
 
-    def increments(half):
+    def increments(half, between):
         cols = pl.ds(half * width, width)
-        acc_ref[...] = jnp.zeros_like(acc_ref)
 
         @pl.loop(0, rows // tb)
         def _(block):
             start = pl.multiple_of(block * tb, tb)
             span = pl.ds(start, tb)
             k = k_ref[span, :]
-            rate = as_column(step_ref[:, span])
-            scaled = (wide(rate, hd) * v_ref[span, :].astype(F32)).astype(BF16)
+            if half == 0:
+                rate = as_column(step_ref[:, span])
+                scaled_ref[span, :] = (wide(rate, hd) * v_ref[span, :].astype(F32)).astype(BF16)
             gate = dotf(k, w_ref[0, :, cols])
             up = dotf(k, w_ref[1, :, cols])
-            back = dotf(scaled, w_ref[2, :, cols])
+            back = dotf(scaled_ref[span, :], w_ref[2, :, cols])
             sig = jax.nn.sigmoid(gate)
             silu = gate * sig
-            hidden = (silu * up).astype(BF16)
-            g_gate = (back * up * (sig * (1.0 + gate * (1.0 - sig)))).astype(BF16)
-            g_up = (back * silu).astype(BF16)
-            acc_ref[:, : 2 * width] += dotf(k, jnp.concatenate([g_gate, g_up], axis=1), TN)
-            acc_ref[:, 2 * width :] += dotf(scaled, hidden, TN)
-
-        for x in range(3):
+            h_ref[span, :] = (silu * up).astype(BF16)
+            g_ref[span, :width] = (back * up * (sig * (1.0 + gate * (1.0 - sig)))).astype(BF16)
+            g_ref[span, width:] = (back * silu).astype(BF16)
+
+        between(0)
+        acc_ref[...] = jnp.zeros_like(acc_ref)
+
+        @pl.loop(0, rows // tb)
+        def _(block):
+            span = pl.ds(pl.multiple_of(block * tb, tb), tb)
+            acc_ref[:, : 2 * width] += dotf(k_ref[span, :], g_ref[span, :], TN)
+
+        hand_on(half, (0, 1))
+        between(1)
+
+        @pl.loop(0, rows // tb)
+        def _(block):
+            span = pl.ds(pl.multiple_of(block * tb, tb), tb)
+            acc_ref[:, 2 * width :] += dotf(scaled_ref[span, :], h_ref[span, :], TN)
+
+        hand_on(half, (2,))
+        between(2)
+
+    def hand_on(half, which):
+        for x in which:
             for part in range(per_half):
                 p = (half * 3 + x) * per_half + part
                 base = x * width + part * PW
@@ -222,8 +248,14 @@
                 jnp.mean(after * after, axis=0, keepdims=True) + EPSILON)
             new_ref[x, :, cols] = (after * rescale).astype(BF16)
 
-    for half in range(2):
-        increments(half)
+    increments(0, lambda step: None)
+    increments(1, chain)
+
+    @pl.when(not_first)
+    def _():
+        for b in late:
+            q_back(b).start()
+
     loads[5].wait()
 
     n_blocks = rows // BQ
@@ -234,9 +266,9 @@
         keys = pl.ds(pl.multiple_of(start - WINDOW, BQ), WINDOW + BQ)
         o, _, l = attend(q_ref[pl.ds(start, BQ), :], k_ref[keys, :], v_ref[keys, :], True, True)
         att_ref[pl.ds(start, BQ), :] = o / l
-        chain(b - halo_blocks)
-
-    t = n_blocks - halo_blocks
+        chain(b - halo_blocks + 3)
+
+    t = n_blocks - halo_blocks + 3
     for b in range(halo_blocks):
         span = pl.ds(b * BQ, BQ)
         keys = pl.ds(0, (b + 1) * BQ)
@@ -247,21 +279,31 @@
         chain(t + b)
     t += halo_blocks
 
-    @pl.when(not_last)
-    def _():
-        q_back().wait_recv()
-        for b in range(halo_blocks):
+    def guest(blocks):
+        for b in blocks:
+            q_back(b).wait_recv()
             span = pl.ds(b * BQ, BQ)
             keys = pl.ds(rows - WINDOW + b * BQ, WINDOW - b * BQ)
             o, m, l = attend(gq_ref[span, :], k_ref[keys, :], v_ref[keys, :], True, False)
             go_ref[span, :] = o.astype(BF16)
             gst_ref[b] = jnp.concatenate([as_row(m), as_row(l), jnp.zeros((6, BQ), F32)], axis=0)
-        o_forward().start()
-        st_forward().start()
+
+    def forward(blocks):
+        for b in blocks:
+            o_forward(b).start()
+            st_forward(b).start()
+
+    @pl.when(not_last)
+    def _():
+        guest(early)
 
     @pl.loop(t, pieces + n_ctx - 2)
     def _(step):
         chain(step)
+
+    @pl.when(not_last)
+    def _():
+        forward(early)
 
     loads[6].wait()
 
@@ -320,12 +362,18 @@
     def _(s):
         apply(halo_chunks + lax.rem(hi + s, rest))
 
-    @pl.when(not_first)
-    def _():
-        o_forward().wait_recv()
-        st_forward().wait_recv()
-
-    for b in range(halo_blocks):
+    @pl.when(not_last)
+    def _():
+        for b in late:
+            guest((b,))
+            forward((b,))
+
+    def combine(b):
+        @pl.when(not_first)
+        def _():
+            o_forward(b).wait_recv()
+            st_forward(b).wait_recv()
+
         span = pl.ds(b * BQ, BQ)
         m1, l1 = stat_ref[0, span, :], stat_ref[1, span, :]
         m2, l2 = as_column(ost_ref[b, :1]), as_column(ost_ref[b, 1:2])
@@ -337,9 +385,12 @@
         att_ref[span, :] = att_ref[span, :] * wide(e1 * inverse, hd) + oin_ref[span, :].astype(F32) * wide(
             e2 * inverse, hd)
 
-    @pl.loop(0, halo_chunks)
-    def _(s):
-        apply(lax.rem(hi + s, halo_chunks))
+    done = halo_blocks
+    for c in range(halo_chunks - 1, -1, -1):
+        while done * BQ > c * per:
+            done -= 1
+            combine(done)
+        apply(jnp.int32(c))
 
     own = pltpu.make_async_copy(z_ref.at[hi], land_ref.at[hi], own_sem.at[0])
     own.start()
@@ -376,7 +427,8 @@
 
     @pl.when(not_first)
     def _():
-        q_back().wait_send()
+        for b in range(halo_blocks):
+            q_back(b).wait_send()
 
         @pl.loop(0, pieces)
         def _(p):
@@ -384,8 +436,9 @@
 
     @pl.when(not_last)
     def _():
-        o_forward().wait_send()
-        st_forward().wait_send()
+        for b in range(halo_blocks):
+            o_forward(b).wait_send()
+            st_forward(b).wait_send()
 
         @pl.loop(0, pieces)
         def _(p):
@@ -412,7 +465,7 @@
         scratch_shapes=[
             V((rows, hd), BF16), V((rows, hd), BF16), V((rows, hd), BF16), V((rows, hd), BF16),
             V((3, hd, fh), BF16), V((3, hd, fh), BF16),
-            V((hd, 3 * fh // 2), F32),
+            V((rows, fh), BF16), V((rows, fh // 2), BF16), V((rows, hd), BF16), V((hd, 3 * fh // 2), F32),
             V((pieces, hd, PW), BF16), V((pieces, hd, PW), BF16), V((pieces, hd, PW), BF16),
             V((pieces, hd, PW), BF16), V((pieces, hd, PW), BF16),
             V((rows, hd), F32), V((2, WINDOW, 128), F32),
@@ -420,7 +473,7 @@
             V((WINDOW, hd), BF16), V((halo_blocks, 8, BQ), F32),
             V((n_head, per, hd), BF16), V((n_head, 8, padded), F32),
             V((n_head, per, hd), BF16), V((n_head, 8, padded), F32),
-            D((7,)), D((pieces,)), D((pieces,)), D((pieces,)), D((pieces,)), D((3,)), D((3,)),
+            D((7,)), D((pieces,)), D((pieces,)), D((pieces,)), D((pieces,)), D((3 * halo_blocks,)), D((3 * halo_blocks,)),
             D((n_head,)), D((n_head,)), D((n_head,)), D((n_head,)), D((2,)), D((n_head,)),
         ],
         compiler_params=pltpu.CompilerParams(

time: 145 us -> 134 us (0.924)
  the two profiles are of different devices: /device:TPU:24 before, /device:TPU:8 now
where the time goes in v1:
time: 134 us; the launch traced here: 133 us
  Pallas kernels  129 us (96%)
  local copies, waits for them, and re-layouts  3.91 us (3%)
    pallas_call x1, Pallas kernels, per_device(): pl.pallas_call(functools.partial(kernel, n_ctx, n_head, rows, hd, fh), ou...  129 us
    unnamed x1, local copies, waits for them, and re-layouts  3.91 us

profile of v1, /device:TPU:8, one launch (start us, length us, event | category | flops | bytes accessed | tf_op | source)
XLA Modules:
  0.0 133.3 jit_solution(10965070857313813841)
XLA Ops:
  0.0 129.4 %shard_map.91 = bf16[384,4096]{1,0:T(8,128)(2,1)} custom-call(bf16[3072,512]{1,0:T(8,128)(2,1)} %q_hbm.1, bf16[3072,512]{1,0:T(8,128)(2,1)} %k_hbm.1, bf16[3072,512]{1,0:T(8,128)(2,1)} %v_hbm.1, f32[1,3072]{1,0:T(1,128)} %step_ref.1, bf16[1,512,512]{2,1,0:T(8,128)(2,1)} %win_hbm.1, bf16[1,512,512]{2,1,0:T(8,128)(2,1)} %wup_hbm.1, ...), custom_call_target="tpu_custom_call" | custom-call | tf_op jit(solution)/shard_map/pallas_call | solution.py:460
  129.4 3.9 %copy.11 = bf16[384,4096]{1,0:T(8,128)(2,1)} copy(bf16[384,4096]{1,0:T(8,128)(2,1)} %shard_map.91) | data formatting | bytes 6291456
